TPU v7x, 32 devices: a whole 2x2x4 slice. The times are simulated.
32 devices in a mesh: blk: 8 (over z, y), fsdp: 4 (over x, core).
Axes of the slice: x: 2, y: 2, z: 4, core: 2. Of those that a mesh axis runs over, the one named last changes fastest.
Arguments:
- tokens: bfloat16 [4, 1024, 768], P('fsdp', 'blk'), may hold values from -6 to 6
- slot_pos: int32 [4, 1024], P('fsdp'), may hold values from 0 to 1023, as said below
- lengths: int32 [4, 4], P('fsdp'), may hold values from 128 to 512, as said below
- thoughts: int32 [4, 64], P('fsdp'), may hold values from 1 to 1023, as said below
- ln_gain: bfloat16 [2, 768], P(None, 'fsdp'), may hold values from 0.5 to 1.5
- ln_shift: bfloat16 [2, 768], P(None, 'fsdp'), may hold values from -2 to 2
- w_qkv: bfloat16 [768, 2304], P('fsdp'), may hold values from -0.21875 to 0.21875
- qv_bias: bfloat16 [2, 768], P(None, 'fsdp'), may hold values from -2 to 2
- w_out: bfloat16 [768, 768], P('fsdp'), may hold values from -0.875 to 0.875
- out_bias: bfloat16 [768], P('fsdp'), may hold values from -2 to 2
- w_fc: bfloat16 [768, 3072], P('fsdp'), may hold values from -0.21875 to 0.21875
- fc_bias: bfloat16 [3072], P('fsdp'), may hold values from -2 to 2
- w_proj: bfloat16 [3072, 768], P('fsdp'), may hold values from -0.109375 to 0.109375
- proj_bias: bfloat16 [768], P('fsdp'), may hold values from -2 to 2
- cotangent: bfloat16 [4, 1024, 768], P('fsdp', 'blk'), may hold values from -6 to 6
Outputs:
- result: bfloat16 [4, 1024, 768], P('fsdp', 'blk')
- grad_tokens: float32 [4, 1024, 768], P('fsdp', 'blk')
- grad_ln_gain: float32 [2, 768], P(None, 'fsdp')
- grad_ln_shift: float32 [2, 768], P(None, 'fsdp')
- grad_w_qkv: float32 [768, 2304], P('fsdp')
- grad_qv_bias: float32 [2, 768], P(None, 'fsdp')
- grad_w_out: float32 [768, 768], P('fsdp')
- grad_out_bias: float32 [768], P('fsdp')
- grad_w_fc: float32 [768, 3072], P('fsdp')
- grad_fc_bias: float32 [3072], P('fsdp')
- grad_w_proj: float32 [3072, 768], P('fsdp')
- grad_proj_bias: float32 [768], P('fsdp')
Inputs may be any that keep to these rules, and one draw needn't show every extreme that they name: In each group slot_pos is a permutation of the group's positions; aligned runs of 8 positions lie together in order on one device of blk, each aligned run of 8 times the number of blk devices positions gives one run to every device, and a device holds its runs in order of position. Each group's 4 lengths sum to 1024; exactly one of them is 512. `thoughts`: 64 distinct positions of the group, none of them 0; positions 1 and 1023 are always among them.
All inputs are finite; a program needn't handle non-finite values.
Results may differ from a plain program's by a relative error of at most 0.015.
Values may be sent and summed in bfloat16 or wider, within the bound.
No kernel may reach another device: no remote copies, remote signals or barrier semaphores. Data moves between devices by JAX's collectives and lax.ppermute only.
A program may use at most 256 MiB of HBM per device.

v0:
```python
import jax
import jax.numpy as jnp
from jax import lax
from jax.sharding import PartitionSpec as P

HEADS = 12
HDIM = 64


epsilon = 1e-05
masked_score = -1e30
highest = lax.Precision.HIGHEST


def gelu_tanh(values):
    return jax.nn.gelu(values, approximate=True)


def layer_norm(inputs, gain, shift):
    center = inputs - jnp.mean(inputs, axis=-1, keepdims=True)
    variance = jnp.mean(center * center, axis=-1, keepdims=True)
    inverse = lax.rsqrt(variance + epsilon)
    scaled = center * inverse
    return (scaled * gain + shift, scaled, inverse)


def norm_back(upstream, scaled, inverse, gain):
    weighted = upstream * gain
    return inverse * (
        weighted
        - jnp.mean(weighted, axis=-1, keepdims=True)
        - scaled * jnp.mean(weighted * scaled, axis=-1, keepdims=True)
    )


def step_size(length):
    candidate = min(length, 512)
    while length % candidate:
        candidate -= 1
    return candidate


def over_blocks(function, carried, length):
    candidate = step_size(length)

    def scan_step(current, number):
        return (function(current, number * candidate, candidate), None)

    return lax.scan(scan_step, carried, jnp.arange(length // candidate, dtype=jnp.int32))[0]


def allowed_pairs(query_pos, query_seq, key_pos, key_seq):
    return (query_seq[:, None] == key_seq[None, :]) & (key_pos[None, :] <= query_pos[:, None])


def block_forward(inputs, weights, layout):
    norm_gains, norm_shifts, w_qkv, qv_bias, w_out, out_bias, w_fc, fc_bias, w_proj, proj_bias = (
        weights
    )
    own_pos, own_seq, group_pos, group_seq = layout
    row_count = inputs.shape[0]
    model_width = HEADS * HDIM
    score_scale = HDIM ** (-0.5)
    normed, scaled_one, inverse_one = layer_norm(
        inputs, norm_gains[0].astype(jnp.float32), norm_shifts[0].astype(jnp.float32)
    )
    normed_low = normed.astype(jnp.bfloat16)
    projected = jnp.dot(normed_low, w_qkv, preferred_element_type=jnp.float32)
    query_rows = (projected[:, :model_width] + qv_bias[0].astype(jnp.float32)).astype(jnp.bfloat16)
    key_rows = projected[:, model_width : 2 * model_width].astype(jnp.bfloat16)
    value_rows = (projected[:, 2 * model_width :] + qv_bias[1].astype(jnp.float32)).astype(
        jnp.bfloat16
    )
    query_heads = query_rows.reshape(row_count, HEADS, HDIM)
    start_state = (
        jnp.full((HEADS, row_count), masked_score, jnp.float32),
        jnp.zeros((HEADS, row_count), jnp.float32),
        jnp.zeros((row_count, HEADS, HDIM), jnp.float32),
    )
    pieces = (
        lax.all_gather(key_rows, "blk", axis=0, tiled=True),
        lax.all_gather(value_rows, "blk", axis=0, tiled=True),
    )
    length = pieces[0].shape[0]
    key_heads = pieces[0].reshape(length, HEADS, HDIM)
    value_heads = pieces[1].reshape(length, HEADS, HDIM)

    def inner_block(current, inner_start, width_now):
        maxima, totals, summed = current
        key_part = lax.dynamic_slice_in_dim(key_heads, inner_start, width_now)
        value_part = lax.dynamic_slice_in_dim(value_heads, inner_start, width_now)
        key_pos = lax.dynamic_slice_in_dim(group_pos, inner_start, width_now)
        key_seq = lax.dynamic_slice_in_dim(group_seq, inner_start, width_now)
        allowed = allowed_pairs(own_pos, own_seq, key_pos, key_seq)[None]
        scores = (
            jnp.einsum("qhd,khd->hqk", query_heads, key_part, preferred_element_type=jnp.float32)
            * score_scale
        )
        scores = jnp.where(allowed, scores, masked_score)
        new_max = jnp.maximum(maxima, jnp.max(scores, axis=-1))
        weights_now = jnp.where(allowed, jnp.exp(scores - new_max[:, :, None]), 0.0)
        factor = jnp.exp(maxima - new_max)
        totals = totals * factor + jnp.sum(weights_now, axis=-1)
        summed = summed * jnp.transpose(factor)[:, :, None] + jnp.einsum(
            "hqk,khd->qhd",
            weights_now.astype(jnp.bfloat16),
            value_part,
            preferred_element_type=jnp.float32,
        )
        return (new_max, totals, summed)

    maxima, totals, summed = over_blocks(inner_block, start_state, length)
    logsum = maxima + jnp.log(totals)
    context = summed / jnp.transpose(totals)[:, :, None]
    context_low = context.reshape(row_count, model_width).astype(jnp.bfloat16)
    middle = inputs + (
        jnp.dot(context_low, w_out, preferred_element_type=jnp.float32)
        + out_bias.astype(jnp.float32)
    )
    second, scaled_two, inverse_two = layer_norm(
        middle, norm_gains[1].astype(jnp.float32), norm_shifts[1].astype(jnp.float32)
    )
    second_low = second.astype(jnp.bfloat16)
    hidden = jnp.dot(second_low, w_fc, preferred_element_type=jnp.float32) + fc_bias.astype(
        jnp.float32
    )
    active_low = gelu_tanh(hidden).astype(jnp.bfloat16)
    output = middle + (
        jnp.dot(active_low, w_proj, preferred_element_type=jnp.float32)
        + proj_bias.astype(jnp.float32)
    )
    kept_state = (
        scaled_one,
        inverse_one,
        normed_low,
        query_rows,
        key_rows,
        value_rows,
        logsum,
        context,
        context_low,
        scaled_two,
        inverse_two,
        second_low,
        hidden,
        active_low,
    )
    return (output, kept_state)


def block_backward(upstream, kept_state, weights, layout):
    norm_gains, norm_shifts, w_qkv, qv_bias, w_out, out_bias, w_fc, fc_bias, w_proj, proj_bias = (
        weights
    )
    (
        scaled_one,
        inverse_one,
        normed_low,
        query_rows,
        key_rows,
        value_rows,
        logsum,
        context,
        context_low,
        scaled_two,
        inverse_two,
        second_low,
        hidden,
        active_low,
    ) = kept_state
    own_pos, own_seq, group_pos, group_seq = layout
    row_count = upstream.shape[0]
    model_width = HEADS * HDIM
    score_scale = HDIM ** (-0.5)
    grad_branch = upstream.astype(jnp.bfloat16)
    grad_w_proj = jnp.einsum(
        "tf,td->fd", active_low, grad_branch, preferred_element_type=jnp.float32
    )
    grad_proj_bias = jnp.sum(grad_branch.astype(jnp.float32), axis=0)
    grad_active = jnp.einsum("td,fd->tf", grad_branch, w_proj, preferred_element_type=jnp.float32)
    grad_hidden = jax.vjp(gelu_tanh, hidden)[1](grad_active)[0].astype(jnp.bfloat16)
    grad_w_fc = jnp.einsum("td,tf->df", second_low, grad_hidden, preferred_element_type=jnp.float32)
    grad_fc_bias = jnp.sum(grad_hidden.astype(jnp.float32), axis=0)
    grad_second = jnp.einsum("tf,df->td", grad_hidden, w_fc, preferred_element_type=jnp.float32)
    grad_gain_two = jnp.sum(grad_second * scaled_two, axis=0)
    grad_shift_two = jnp.sum(grad_second, axis=0)
    grad_middle = upstream + norm_back(
        grad_second, scaled_two, inverse_two, norm_gains[1].astype(jnp.float32)
    )
    grad_attn = grad_middle.astype(jnp.bfloat16)
    grad_w_out = jnp.einsum("te,td->ed", context_low, grad_attn, preferred_element_type=jnp.float32)
    grad_out_bias = jnp.sum(grad_attn.astype(jnp.float32), axis=0)
    grad_context = jnp.einsum(
        "td,ed->te", grad_attn, w_out, preferred_element_type=jnp.float32
    ).astype(jnp.bfloat16)
    grad_heads = grad_context.reshape(row_count, HEADS, HDIM)
    query_heads = query_rows.reshape(row_count, HEADS, HDIM)
    own_keys = key_rows.reshape(row_count, HEADS, HDIM)
    own_values = value_rows.reshape(row_count, HEADS, HDIM)
    delta = jnp.transpose(jnp.sum(grad_heads.astype(jnp.float32) * context, axis=-1))
    all_logsum, all_delta = (
        lax.all_gather(logsum, "blk", axis=1, tiled=True),
        lax.all_gather(delta, "blk", axis=1, tiled=True),
    )
    pieces = (
        lax.all_gather(key_rows, "blk", axis=0, tiled=True),
        lax.all_gather(value_rows, "blk", axis=0, tiled=True),
    )
    length = pieces[0].shape[0]
    key_heads = pieces[0].reshape(length, HEADS, HDIM)
    value_heads = pieces[1].reshape(length, HEADS, HDIM)

    def inner_block(current, inner_start, width_now):
        key_part = lax.dynamic_slice_in_dim(key_heads, inner_start, width_now)
        value_part = lax.dynamic_slice_in_dim(value_heads, inner_start, width_now)
        key_pos = lax.dynamic_slice_in_dim(group_pos, inner_start, width_now)
        key_seq = lax.dynamic_slice_in_dim(group_seq, inner_start, width_now)
        allowed = allowed_pairs(own_pos, own_seq, key_pos, key_seq)[None]
        scores = (
            jnp.einsum("qhd,khd->hqk", query_heads, key_part, preferred_element_type=jnp.float32)
            * score_scale
        )
        probability = jnp.where(allowed, jnp.exp(scores - logsum[:, :, None]), 0.0)
        grad_probs = jnp.einsum(
            "qhd,khd->hqk", grad_heads, value_part, preferred_element_type=jnp.float32
        )
        grad_scores = (probability * (grad_probs - delta[:, :, None])).astype(jnp.bfloat16)
        return (
            current
            + jnp.einsum("hqk,khd->qhd", grad_scores, key_part, preferred_element_type=jnp.float32)
            * score_scale
        )

    grad_query = over_blocks(inner_block, jnp.zeros((row_count, HEADS, HDIM), jnp.float32), length)
    zero_heads = jnp.zeros((row_count, HEADS, HDIM), jnp.float32)
    pieces = (
        lax.all_gather(query_rows, "blk", axis=0, tiled=True),
        lax.all_gather(grad_context, "blk", axis=0, tiled=True),
    )
    length = pieces[0].shape[0]
    remote_queries = pieces[0].reshape(length, HEADS, HDIM)
    remote_grads = pieces[1].reshape(length, HEADS, HDIM)

    def inner_block(current, inner_start, width_now):
        grad_keys, grad_values = current
        query_part = lax.dynamic_slice_in_dim(remote_queries, inner_start, width_now)
        grad_part = lax.dynamic_slice_in_dim(remote_grads, inner_start, width_now)
        query_pos = lax.dynamic_slice_in_dim(group_pos, inner_start, width_now)
        query_seq = lax.dynamic_slice_in_dim(group_seq, inner_start, width_now)
        logsum_part = lax.dynamic_slice_in_dim(all_logsum, inner_start, width_now, axis=1)
        delta_part = lax.dynamic_slice_in_dim(all_delta, inner_start, width_now, axis=1)
        allowed = allowed_pairs(query_pos, query_seq, own_pos, own_seq)[None]
        scores = (
            jnp.einsum("qhd,khd->hqk", query_part, own_keys, preferred_element_type=jnp.float32)
            * score_scale
        )
        probability = jnp.where(allowed, jnp.exp(scores - logsum_part[:, :, None]), 0.0)
        grad_values = grad_values + jnp.einsum(
            "hqk,qhd->khd",
            probability.astype(jnp.bfloat16),
            grad_part,
            preferred_element_type=jnp.float32,
        )
        grad_probs = jnp.einsum(
            "qhd,khd->hqk", grad_part, own_values, preferred_element_type=jnp.float32
        )
        grad_scores = (probability * (grad_probs - delta_part[:, :, None])).astype(jnp.bfloat16)
        grad_keys = (
            grad_keys
            + jnp.einsum(
                "hqk,qhd->khd", grad_scores, query_part, preferred_element_type=jnp.float32
            )
            * score_scale
        )
        return (grad_keys, grad_values)

    grad_keys, grad_values = over_blocks(inner_block, (zero_heads, zero_heads), length)
    grad_q_low = grad_query.reshape(row_count, model_width).astype(jnp.bfloat16)
    grad_k_low = grad_keys.reshape(row_count, model_width).astype(jnp.bfloat16)
    grad_v_low = grad_values.reshape(row_count, model_width).astype(jnp.bfloat16)
    grad_projected = jnp.concatenate([grad_q_low, grad_k_low, grad_v_low], axis=1)
    grad_w_qkv = jnp.einsum(
        "td,te->de", normed_low, grad_projected, preferred_element_type=jnp.float32
    )
    grad_qv_bias = jnp.stack(
        [
            jnp.sum(grad_q_low.astype(jnp.float32), axis=0),
            jnp.sum(grad_v_low.astype(jnp.float32), axis=0),
        ]
    )
    grad_normed = jnp.einsum("te,de->td", grad_projected, w_qkv, preferred_element_type=jnp.float32)
    grad_gain_one = jnp.sum(grad_normed * scaled_one, axis=0)
    grad_shift_one = jnp.sum(grad_normed, axis=0)
    grad_inputs = grad_middle + norm_back(
        grad_normed, scaled_one, inverse_one, norm_gains[0].astype(jnp.float32)
    )
    gradients = (
        jnp.stack([grad_gain_one, grad_gain_two]),
        jnp.stack([grad_shift_one, grad_shift_two]),
        grad_w_qkv,
        grad_qv_bias,
        grad_w_out,
        grad_out_bias,
        grad_w_fc,
        grad_fc_bias,
        grad_w_proj,
        grad_proj_bias,
    )
    return (grad_inputs, gradients)


def reduce_once(gradients):
    shards = (
        lax.psum_scatter(
            gradients[0].astype(jnp.bfloat16), "fsdp", scatter_dimension=1, tiled=True
        ).astype(jnp.float32),
        lax.psum_scatter(
            gradients[1].astype(jnp.bfloat16), "fsdp", scatter_dimension=1, tiled=True
        ).astype(jnp.float32),
        lax.psum_scatter(
            gradients[2].astype(jnp.bfloat16), "fsdp", scatter_dimension=0, tiled=True
        ).astype(jnp.float32),
        lax.psum_scatter(
            gradients[3].astype(jnp.bfloat16), "fsdp", scatter_dimension=1, tiled=True
        ).astype(jnp.float32),
        lax.psum_scatter(
            gradients[4].astype(jnp.bfloat16), "fsdp", scatter_dimension=0, tiled=True
        ).astype(jnp.float32),
        lax.psum_scatter(
            gradients[5].astype(jnp.bfloat16), "fsdp", scatter_dimension=0, tiled=True
        ).astype(jnp.float32),
        lax.psum_scatter(
            gradients[6].astype(jnp.bfloat16), "fsdp", scatter_dimension=0, tiled=True
        ).astype(jnp.float32),
        lax.psum_scatter(
            gradients[7].astype(jnp.bfloat16), "fsdp", scatter_dimension=0, tiled=True
        ).astype(jnp.float32),
        lax.psum_scatter(
            gradients[8].astype(jnp.bfloat16), "fsdp", scatter_dimension=0, tiled=True
        ).astype(jnp.float32),
        lax.psum_scatter(
            gradients[9].astype(jnp.bfloat16), "fsdp", scatter_dimension=0, tiled=True
        ).astype(jnp.float32),
    )
    return lax.psum(shards, "blk")


def local(
    tokens,
    slot_pos,
    lengths,
    thoughts,
    ln_gain,
    ln_shift,
    w_qkv,
    qv_bias,
    w_out,
    out_bias,
    w_fc,
    fc_bias,
    w_proj,
    proj_bias,
    cotangent,
):
    weights = (
        lax.all_gather(ln_gain, "fsdp", axis=1, tiled=True),
        lax.all_gather(ln_shift, "fsdp", axis=1, tiled=True),
        lax.all_gather(w_qkv, "fsdp", axis=0, tiled=True),
        lax.all_gather(qv_bias, "fsdp", axis=1, tiled=True),
        lax.all_gather(w_out, "fsdp", axis=0, tiled=True),
        lax.all_gather(out_bias, "fsdp", axis=0, tiled=True),
        lax.all_gather(w_fc, "fsdp", axis=0, tiled=True),
        lax.all_gather(fc_bias, "fsdp", axis=0, tiled=True),
        lax.all_gather(w_proj, "fsdp", axis=0, tiled=True),
        lax.all_gather(proj_bias, "fsdp", axis=0, tiled=True),
    )
    row_count = tokens.shape[1]
    blk_index = lax.axis_index("blk")
    group_pos = slot_pos[0]
    seq_ends = jnp.cumsum(lengths[0])
    group_seq = jnp.sum((group_pos[:, None] >= seq_ends[None, :]).astype(jnp.int32), axis=1)
    own_pos = lax.dynamic_slice_in_dim(group_pos, blk_index * row_count, row_count)
    own_seq = lax.dynamic_slice_in_dim(group_seq, blk_index * row_count, row_count)
    layout = (own_pos, own_seq, group_pos, group_seq)
    latent_in = tokens[0].astype(jnp.float32)
    latent_out, latent_state = block_forward(latent_in, weights, layout)
    source = (own_pos[None, :] == thoughts[0][:, None] - 1).astype(jnp.float32)
    target = (own_pos[None, :] == thoughts[0][:, None]).astype(jnp.float32)
    carried = lax.psum(jnp.dot(source, latent_out, precision=highest), "blk")
    keep_rows = 1.0 - jnp.sum(target, axis=0)
    token_in = latent_in * keep_rows[:, None] + jnp.einsum(
        "nt,nd->td", target, carried, precision=highest
    )
    token_out, token_state = block_forward(token_in, weights, layout)
    upstream = cotangent[0].astype(jnp.float32)
    token_grad, token_grads = block_backward(upstream, token_state, weights, layout)
    thought_back = lax.psum(jnp.dot(target, token_grad, precision=highest), "blk")
    latent_upstream = jnp.einsum("nt,nd->td", source, thought_back, precision=highest)
    latent_grad, latent_grads = block_backward(latent_upstream, latent_state, weights, layout)
    input_grad = token_grad * keep_rows[:, None] + latent_grad
    reduced = reduce_once(
        tuple(
            (first_part + second_part for first_part, second_part in zip(token_grads, latent_grads))
        )
    )
    return (
        token_out.astype(jnp.bfloat16)[None],
        input_grad[None],
        reduced[0],
        reduced[1],
        reduced[2],
        reduced[3],
        reduced[4],
        reduced[5],
        reduced[6],
        reduced[7],
        reduced[8],
        reduced[9],
    )


def solution(mesh):
    return jax.shard_map(
        local,
        mesh=mesh,
        in_specs=(
            P("fsdp", "blk", None),
            P("fsdp", None),
            P("fsdp", None),
            P("fsdp", None),
            P(None, "fsdp"),
            P(None, "fsdp"),
            P("fsdp", None),
            P(None, "fsdp"),
            P("fsdp", None),
            P("fsdp"),
            P("fsdp", None),
            P("fsdp"),
            P("fsdp", None),
            P("fsdp"),
            P("fsdp", "blk", None),
        ),
        out_specs=(
            P("fsdp", "blk", None),
            P("fsdp", "blk", None),
            P(None, "fsdp"),
            P(None, "fsdp"),
            P("fsdp", None),
            P(None, "fsdp"),
            P("fsdp", None),
            P("fsdp"),
            P("fsdp", None),
            P("fsdp"),
            P("fsdp", None),
            P("fsdp"),
        ),
        check_vma=False,
    )
```

profile of v0, /device:TPU:0, one launch (start us, length us, event | category | flops | bytes accessed | tf_op | source)
XLA Modules:
  0.0 1328.6 jit_solution(10846110797163329717)
XLA Ops:
  8.0 6.3 all-gather.1
  14.3 5.5 all-gather
  22.2 20.8 %all-gather.17.cloned.1.call-done = bf16[768,2304]{1,0:T(8,128)(2,1)} async-done(((bf16[192,2304]{1,0:T(8,128)(2,1)}), bf16[768,2304]{1,0:T(8,128)(2,1)}) %all-gather.17.cloned.1.call-update) | async-done | bytes 3538960 | tf_op jit(solution)/shard_map/all_gather | solution.py:368
  56.3 6.2 all-reduce.7
  62.7 5.2 all-gather.3
  69.3 21.7 %all-gather.19.cloned.1.call-done = bf16[1024,768]{1,0:T(8,128)(2,1)} async-done(((bf16[128,768]{1,0:T(8,128)(2,1)}), bf16[1024,768]{1,0:T(8,128)(2,1)}) %all-gather.19.cloned.1.call-update) | async-done | bytes 1572880 | tf_op jit(solution)/shard_map/all_gather | solution.py:81
  93.6 43.2 %all-gather.21.cloned.1.call-done = bf16[1024,768]{1,0:T(8,128)(2,1)} async-done(((bf16[128,768]{1,0:T(8,128)(2,1)}), bf16[1024,768]{1,0:T(8,128)(2,1)}) %all-gather.21.cloned.1.call-update) | async-done | bytes 1572880 | tf_op jit(solution)/shard_map/all_gather | solution.py:82
  139.4 15.2 %while.78 = (s32[]{:T(128)}, f32[12,128]{1,0:T(8,128)S(1)}, f32[12,128]{1,0:T(8,128)S(1)}, f32[128,12,64]{0,2,1:T(8,128)}, s32[128]{0:T(128)}, /*index=5*/s32[2]...) while((s32[]{:T(128)}, f32[12,128]{1,0:T(8,128)S(1)}, ...), condition=%wide.region_8.9_spmd.clone, body=%wide.region_5.8_spmd.clone.sunk | while | flops 212050944 | bytes 21808456 | solution.py:49
  157.7 35.7 %all-gather.25.cloned.1.call-done = bf16[768,3072]{1,0:T(8,128)(2,1)} async-done(((bf16[192,3072]{1,0:T(8,128)(2,1)}), bf16[768,3072]{1,0:T(8,128)(2,1)}) %all-gather.25.cloned.1.call-update) | async-done | bytes 4718608 | tf_op jit(solution)/shard_map/all_gather | solution.py:372
  196.7 35.7 %all-gather.27.cloned.1.call-done = bf16[3072,768]{1,0:T(8,128)(2,1)} async-done(((bf16[768,768]{1,0:T(8,128)(2,1)}), bf16[3072,768]{1,0:T(8,128)(2,1)}) %all-gather.27.cloned.1.call-update) | async-done | bytes 4718608 | tf_op jit(solution)/shard_map/all_gather | solution.py:374
  239.0 68.6 %all-reduce.12.cloned.1.call-done = f32[64,768]{1,0:T(8,128)} async-done(((f32[64,768]{1,0:T(8,128)}), f32[64,768]{1,0:T(8,128)}) %all-reduce.12.cloned.1.call-update) | async-done | bytes 196624 | tf_op jit(solution)/shard_map/psum | solution.py:389
  315.4 37.9 %all-gather.37.cloned.1.call-done = bf16[1024,768]{1,0:T(8,128)(2,1)} async-done(((bf16[128,768]{1,0:T(8,128)(2,1)}), bf16[1024,768]{1,0:T(8,128)(2,1)}) %all-gather.37.cloned.1.call-update) | async-done | bytes 1572880 | tf_op jit(solution)/shard_map/all_gather | solution.py:237
  356.4 42.3 %all-gather.29.cloned.1.call-done = bf16[1024,768]{1,0:T(8,128)(2,1)} async-done(((bf16[128,768]{1,0:T(8,128)(2,1)}), bf16[1024,768]{1,0:T(8,128)(2,1)}) %all-gather.29.cloned.1.call-update) | async-done | bytes 1572880 | tf_op jit(solution)/shard_map/all_gather | solution.py:81
  401.3 42.7 %all-gather.31.cloned.1.call-done = bf16[1024,768]{1,0:T(8,128)(2,1)} async-done(((bf16[128,768]{1,0:T(8,128)(2,1)}), bf16[1024,768]{1,0:T(8,128)(2,1)}) %all-gather.31.cloned.1.call-update) | async-done | bytes 1572880 | tf_op jit(solution)/shard_map/all_gather | solution.py:82
  447.2 21.0 %while.79 = (s32[]{:T(128)}, f32[12,128]{1,0:T(8,128)}, f32[12,128]{1,0:T(8,128)}, f32[128,12,64]{0,2,1:T(8,128)}, s32[128]{0:T(128)}, /*index=5*/s32[2]{0:T(128...) while((s32[]{:T(128)}, f32[12,128]{1,0:T(8,128)}, ...), condition=%wide.region_17.18_spmd.clone, body=%wide.region_14.17_spmd.clone.sunk | while | flops 212050944 | bytes 22406612 | solution.py:49
  482.9 32.7 %all_gather.89 = f32[12,1024]{1,0:T(8,128)} all-gather(f32[12,128]{1,0:T(8,128)S(1)} %log_add_fusion), channel_id=1, replica_groups=mesh['blk'=8,'fsdp'=4] {'blk'}, dimensions={1}, use_global_device_ids=true | all-gather | bytes 55296 | tf_op jit(solution)/shard_map/all_gather | solution.py:202
  522.2 32.7 %all_gather.85 = f32[12,1024]{1,0:T(8,128)} all-gather(f32[12,128]{1,0:T(8,128)} %log_add_fusion.1), channel_id=1, replica_groups=mesh['blk'=8,'fsdp'=4] {'blk'}, dimensions={1}, use_global_device_ids=true | all-gather | bytes 55296 | tf_op jit(solution)/shard_map/all_gather | solution.py:202
  555.9 32.9 %all_gather.87 = f32[12,1024]{1,0:T(8,128)} all-gather(f32[12,128]{1,0:T(8,128)S(1)} %bitcast.399), channel_id=1, replica_groups=mesh['blk'=8,'fsdp'=4] {'blk'}, dimensions={1}, use_global_device_ids=true | all-gather | bytes 55296 | tf_op jit(solution)/shard_map/all_gather | solution.py:203
  589.3 18.0 %while.80 = (s32[]{:T(128)}, f32[128,12,64]{0,2,1:T(8,128)}, s32[2]{0:T(128)}, bf16[1024,12,64]{0,2,1:T(8,128)(2,1)}, s32[128]{0:T(128)}, /*index=5*/s32[1024]{0...) while((s32[]{:T(128)}, f32[128,12,64]{0,2,1:T(8,128)}, ...), condition=%wide.region_24.25_spmd.clone, body=%wide.region_23.24_spmd.clone.sunk | while | flops 307200000 | bytes 9990900 | solution.py:49
  612.2 26.3 %while.81 = (s32[]{:T(128)}, f32[128,12,64]{0,2,1:T(8,128)}, f32[128,12,64]{0,2,1:T(8,128)}, s32[2]{0:T(128)S(1)}, bf16[1024,12,64]{0,2,1:T(8,128)(2,1)}, /*inde...) while((s32[]{:T(128)}, f32[128,12,64]{0,2,1:T(8,128)}, ...), condition=%wide.region_26.27_spmd.clone, body=%wide.region_25.26_spmd.clone.sunk | while | flops 411205632 | bytes 15350709 | solution.py:49
  648.3 5.2 fusion.232
  653.4 63.5 %all-reduce.14.cloned.1.call-done = f32[64,768]{1,0:T(8,128)} async-done(((f32[64,768]{1,0:T(8,128)}), f32[64,768]{1,0:T(8,128)}) %all-reduce.14.cloned.1.call-update) | async-done | bytes 196624 | tf_op jit(solution)/shard_map/psum | solution.py:397
  740.2 18.3 %while.82 = (s32[]{:T(128)}, f32[128,12,64]{0,2,1:T(8,128)}, s32[2]{0:T(128)}, bf16[1024,12,64]{0,2,1:T(8,128)(2,1)}, s32[128]{0:T(128)}, /*index=5*/s32[1024]{0...) while((s32[]{:T(128)}, f32[128,12,64]{0,2,1:T(8,128)}, ...), condition=%wide.region_34.35_spmd.clone, body=%wide.region_33.34_spmd.clone.sunk | while | flops 307200000 | bytes 9992948 | solution.py:49
  760.9 32.4 %all_gather.91 = f32[12,1024]{1,0:T(8,128)} all-gather(f32[12,128]{1,0:T(8,128)} %get-tuple-element.1960), channel_id=1, replica_groups=mesh['blk'=8,'fsdp'=4] {'blk'}, dimensions={1}, use_global_device_ids=true | all-gather | bytes 55296 | tf_op jit(solution)/shard_map/all_gather | solution.py:203
  800.0 27.7 %while.83 = (s32[]{:T(128)}, f32[128,12,64]{0,2,1:T(8,128)}, f32[128,12,64]{0,2,1:T(8,128)}, s32[2]{0:T(128)}, bf16[1024,12,64]{0,2,1:T(8,128)(2,1)}, /*index=5*...) while((s32[]{:T(128)}, f32[128,12,64]{0,2,1:T(8,128)}, ...), condition=%wide.region_36.37_spmd.clone, body=%wide.region_35.36_spmd.clone.sunk | while | flops 411205632 | bytes 15350589 | solution.py:49
  837.3 7.4 add_convert_fusion.1
  862.9 10.1 all-reduce.6
  876.9 21.3 %reduce-scatter.26.cloned.1.call-done = bf16[192,2]{1,0:T(8,128)(2,1)} async-done(((bf16[768,2]{1,0:T(8,128)(2,1)}), bf16[192,2]{1,0:T(8,128)(2,1)}) %reduce-scatter.26.cloned.1.call-update) | async-done | bytes 784
  899.1 49.7 %reduce-scatter.18.cloned.1.call-done = bf16[192,3072]{1,0:T(8,128)(2,1)} async-done(((bf16[768,3072]{1,0:T(8,128)(2,1)}), bf16[192,3072]{1,0:T(8,128)(2,1)}) %reduce-scatter.18.cloned.1.call-update) | async-done | bytes 1179664 | tf_op jit(solution)/shard_map/reduce_scatter | solution.py:332
  948.8 50.3 %reduce-scatter.20.cloned.1.call-done = bf16[768,768]{1,0:T(8,128)(2,1)} async-done(((bf16[3072,768]{1,0:T(8,128)(2,1)}), bf16[768,768]{1,0:T(8,128)(2,1)}) %reduce-scatter.20.cloned.1.call-update) | async-done | bytes 1179664 | tf_op jit(solution)/shard_map/reduce_scatter | solution.py:338
  999.1 43.2 %reduce-scatter.14.cloned.1.call-done = bf16[192,2304]{1,0:T(8,128)(2,1)} async-done(((bf16[768,2304]{1,0:T(8,128)(2,1)}), bf16[192,2304]{1,0:T(8,128)(2,1)}) %reduce-scatter.14.cloned.1.call-update) | async-done | bytes 884752 | tf_op jit(solution)/shard_map/reduce_scatter | solution.py:320
  1042.3 279.1 %all-reduce.15 = (f32[2,192]{1,0:T(2,128)}, f32[2,192]{1,0:T(2,128)}, f32[192,2304]{1,0:T(8,128)}, f32[2,192]{1,0:T(2,128)}, f32[192,768]{1,0:T(8,128)}, /*index...) all-reduce(bf16[2,192]{1,0:T(2,128)(2,1)S(1)} %copy.127, ...), channel_id=1, replica_groups=mesh['blk'=8,'fsdp'=4] {'blk'}, use_global_device_ids=true, to_apply=%region_44.45 | all-reduce | flops 1771776 | bytes 10632960 | tf_op jit(solution)/shard_map/psum | solution.py:345
  (635 shorter events, 269.4 us)
Async XLA Ops:
  7.2 35.9 %all-gather.17.cloned.1.call-start = ((), (), s32[]{:S(2)}) async-start(), calls=%async_computation.7 | async-start | bytes 4423680 | tf_op jit(solution)/shard_map/all_gather | solution.py:368
  7.9 83.1 %all-gather.19.cloned.1.call-start = ((), (), s32[]{:S(2)}) async-start(), calls=%async_computation.8 | async-start | bytes 1769472 | tf_op jit(solution)/shard_map/all_gather | solution.py:81
  19.9 173.5 %copy-start.83 = (f32[768]{0:T(1024)}, f32[768]{0:T(1024)S(1)}, u32[]{:S(2)}) copy-start(f32[768]{0:T(1024)S(1)} %get-tuple-element.834) | copy-start | bytes 9220
  19.9 289.4 %copy-start.81 = (f32[768]{0:T(1024)}, f32[768]{0:T(1024)S(1)}, u32[]{:S(2)}) copy-start(f32[768]{0:T(1024)S(1)} %get-tuple-element.835) | copy-start | bytes 9220
  20.0 173.5 %copy-start.68 = (f32[768]{0:T(1024)}, f32[768]{0:T(1024)S(1)}, u32[]{:S(2)}) copy-start(f32[768]{0:T(1024)S(1)} %get-tuple-element.832) | copy-start | bytes 9220
  20.0 289.3 %copy-start.77 = (f32[768]{0:T(1024)}, f32[768]{0:T(1024)S(1)}, u32[]{:S(2)}) copy-start(f32[768]{0:T(1024)S(1)} %get-tuple-element.833) | copy-start | bytes 9220
  46.6 90.2 %all-gather.21.cloned.1.call-start = ((), (), s32[]{:S(2)}) async-start(), calls=%async_computation.9 | async-start | bytes 1769472 | tf_op jit(solution)/shard_map/all_gather | solution.py:82
  52.7 103.0 %all-gather.23.cloned.1.call-start = ((), (), s32[]{:S(2)}) async-start(), calls=%async_computation.10 | async-start | bytes 1474560 | tf_op jit(solution)/shard_map/all_gather | solution.py:370
  53.3 140.2 %all-gather.25.cloned.1.call-start = ((), (), s32[]{:S(2)}) async-start(), calls=%async_computation.11 | async-start | bytes 5898240 | tf_op jit(solution)/shard_map/all_gather | solution.py:372
  53.9 178.5 %all-gather.27.cloned.1.call-start = ((), (), s32[]{:S(2)}) async-start(), calls=%async_computation.12 | async-start | bytes 5898240 | tf_op jit(solution)/shard_map/all_gather | solution.py:374
  54.5 253.2 %all-reduce.12.cloned.1.call-start = ((), (), s32[]{:S(2)}) async-start(), calls=%async_computation.13 | async-start | bytes 393216 | tf_op jit(solution)/shard_map/psum | solution.py:389
  62.5 93.2 %copy-start.89 = (f32[768]{0:T(1024)}, f32[768]{0:T(1024)S(1)}, u32[]{:S(2)}) copy-start(f32[768]{0:T(1024)S(1)} %convert_element_type.290) | copy-start | bytes 9220
  62.7 169.6 %copy-start.132 = (f32[768]{0:T(1024)}, f32[768]{0:T(1024)S(1)}, u32[]{:S(2)}) copy-start(f32[768]{0:T(1024)S(1)} %convert_element_type.294) | copy-start | bytes 9220
  67.9 125.5 %copy-start.87 = (f32[4,1,768]{2,1,0:T(1,128)}, f32[4,1,768]{2,1,0:T(1,128)S(1)}, u32[]{:S(2)}) copy-start(f32[4,1,768]{2,1,0:T(1,128)S(1)} %convert_element_type.354) | copy-start | bytes 36868
  69.1 166.6 %copy-start.138 = (s32[64]{0:T(128)}, s32[64]{0:T(128)S(1)}, u32[]{:S(2)}) copy-start(s32[64]{0:T(128)S(1)} %broadcast_add_fusion) | copy-start | bytes 772
  157.5 74.9 %copy-start.10 = (f32[128,768]{1,0:T(8,128)}, f32[128,768]{1,0:T(8,128)S(1)}, u32[]{:S(2)}) copy-start(f32[128,768]{1,0:T(8,128)S(1)} %get-tuple-element.1042) | copy-start | bytes 1179652
  196.7 110.9 %copy-start.13 = (bf16[1,128,768]{2,1,0:T(8,128)(2,1)S(1)}, bf16[1,128,768]{2,1,0:T(8,128)(2,1)}, u32[]{:S(2)}) copy-start(bf16[1,128,768]{2,1,0:T(8,128)(2,1)} %param.27) | copy-start | bytes 589828
  237.4 115.9 %all-gather.37.cloned.1.call-start = ((), (), s32[]{:S(2)}) async-start(), calls=%async_computation.19 | async-start | bytes 1769472 | tf_op jit(solution)/shard_map/all_gather | solution.py:237
  238.2 160.6 %all-gather.29.cloned.1.call-start = ((), (), s32[]{:S(2)}) async-start(), calls=%async_computation.14 | async-start | bytes 1769472 | tf_op jit(solution)/shard_map/all_gather | solution.py:81
  312.8 131.2 %all-gather.31.cloned.1.call-start = ((), (), s32[]{:S(2)}) async-start(), calls=%async_computation.15 | async-start | bytes 1769472 | tf_op jit(solution)/shard_map/all_gather | solution.py:82
  313.6 205.3 %all-gather.33.cloned.1.call-start = ((), (), s32[]{:S(2)}) async-start(), calls=%async_computation.16 | async-start | bytes 1769472 | tf_op jit(solution)/shard_map/all_gather | solution.py:237
  356.2 253.4 %all-gather.35.cloned.1.call-start = ((), (), s32[]{:S(2)}) async-start(), calls=%async_computation.17 | async-start | bytes 1769472 | tf_op jit(solution)/shard_map/all_gather | solution.py:238
  482.8 234.2 %all-reduce.14.cloned.1.call-start = ((), (), s32[]{:S(2)}) async-start(), calls=%async_computation.18 | async-start | bytes 393216 | tf_op jit(solution)/shard_map/psum | solution.py:397
  648.0 148.9 %all-gather.39.cloned.1.call-start = ((), (), s32[]{:S(2)}) async-start(), calls=%async_computation.20 | async-start | bytes 1769472 | tf_op jit(solution)/shard_map/all_gather | solution.py:238
  730.5 142.8 %reduce-scatter.16.cloned.1.call-start = ((), (), s32[]{:S(2)}) async-start(), calls=%async_computation.22 | async-start | bytes 1474560 | tf_op jit(solution)/shard_map/reduce_scatter | solution.py:326
  796.7 77.6 %reduce-scatter.22.cloned.1.call-start = ((), (), s32[]{:S(2)}) async-start(), calls=%async_computation.25 | async-start | bytes 245760
  835.1 40.9 %reduce-scatter.24.cloned.1.call-start = ((), (), s32[]{:S(2)}) async-start(), calls=%async_computation.26 | async-start | bytes 245760
  836.2 62.0 %reduce-scatter.26.cloned.1.call-start = ((), (), s32[]{:S(2)}) async-start(), calls=%async_computation.27 | async-start | bytes 245760
  837.2 111.6 %reduce-scatter.18.cloned.1.call-start = ((), (), s32[]{:S(2)}) async-start(), calls=%async_computation.23 | async-start | bytes 5898240 | tf_op jit(solution)/shard_map/reduce_scatter | solution.py:332
  844.7 154.4 %reduce-scatter.20.cloned.1.call-start = ((), (), s32[]{:S(2)}) async-start(), calls=%async_computation.24 | async-start | bytes 5898240 | tf_op jit(solution)/shard_map/reduce_scatter | solution.py:338
  851.7 190.6 %reduce-scatter.14.cloned.1.call-start = ((), (), s32[]{:S(2)}) async-start(), calls=%async_computation.21 | async-start | bytes 4423680 | tf_op jit(solution)/shard_map/reduce_scatter | solution.py:320
  873.3 169.0 %copy-start.80 = (bf16[192,768]{1,0:T(8,128)(2,1)S(1)}, bf16[192,768]{1,0:T(8,128)(2,1)}, u32[]{:S(2)}) copy-start(bf16[192,768]{1,0:T(8,128)(2,1)} %reduce-scatter.16.cloned.1.call-done) | copy-start | bytes 884740
  (157 other events, 1302.9 us)
Sparse Core Ops, SparseCore 0:
  9.6 33.4 all-gather.16
  46.8 44.2 all-gather.18
  93.8 42.9 all-gather.20
  138.2 16.2 all-gather.22
  155.9 37.4 all-gather.24
  194.9 37.4 all-gather.26
  237.5 70.0 all-reduce.11
  310.0 43.2 all-gather.36
  355.7 42.9 all-gather.28
  401.0 42.9 all-gather.30
  446.5 43.0 all-gather.32
  492.4 43.7 all-gather.34
  648.1 68.8 all-reduce.13
  730.6 43.5 all-gather.38
  796.8 24.0 reduce-scatter.15
  835.3 17.9 reduce-scatter.21
  856.2 19.7 reduce-scatter.23
  878.5 19.6 reduce-scatter.25
  900.9 47.8 reduce-scatter.17
  951.2 47.8 reduce-scatter.19
  1001.8 40.4 reduce-scatter.13
where the time goes:
time: 1340 us; the launch traced here: 1330 us
  waiting for transfers between devices  581 us (43%)
  blocking collectives  448 us (33%)
  matrix products  156 us (12%)
  local copies, waits for them, and re-layouts  70.4 us (5%)
  other arithmetic  44.8 us (3%)
  between operations  18.7 us (1%)
    psum x1, blocking collectives, reduce_once(): return lax.psum(shards, 'blk')  279 us
    all_gather x2, waiting for transfers between devices, block_forward(): lax.all_gather(value_rows, 'blk', axis=0, tiled=True)  85.9 us
    psum x1, waiting for transfers between devices, local(): carried = lax.psum(jnp.dot(source, latent_out, precision=highest), 'blk')  68.6 us
    all_gather x2, blocking collectives, block_backward(): lax.all_gather(logsum, 'blk', axis=1, tiled=True)  65.3 us
    all_gather x2, blocking collectives, block_backward(): lax.all_gather(delta, 'blk', axis=1, tiled=True)  65.3 us
    all_gather x2, waiting for transfers between devices, block_forward(): lax.all_gather(key_rows, 'blk', axis=0, tiled=True)  64.1 us
    psum x1, waiting for transfers between devices, local(): lax.psum(jnp.dot(target, token_grad, precision=highest), 'blk')  63.5 us
    reduce_scatter x1, waiting for transfers between devices, reduce_once(): lax.psum_scatter(gradients[8].astype(jnp.bfloat16), 'fsdp', scatter_dimen...  50.3 us
  transfers between devices with their start and end apart: 21, of which 15 were waited for; matrix products, arithmetic and copies ran while one was open for 15% of the time, Pallas kernels for 0%

commit v1 on v0

v1 whole, which is shorter than its diff:
```python
import jax
import jax.numpy as jnp
from jax import lax
from jax.sharding import PartitionSpec as P

HDIM = 64
PARTS = 4
EPS = 1e-05
SCALE = HDIM ** (-0.5)
F32 = jnp.float32
BF16 = jnp.bfloat16


def dot(a, b, ca=1, cb=0):
    return lax.dot_general(a, b, (((ca,), (cb,)), ((), ())), preferred_element_type=F32)


def exact(a, b, ca=1, cb=0):
    return lax.dot_general(
        a, b, (((ca,), (cb,)), ((), ())), precision=lax.Precision.HIGHEST, preferred_element_type=F32
    )


def norm(x, gain, shift):
    center = x - jnp.mean(x, axis=-1, keepdims=True)
    inverse = lax.rsqrt(jnp.mean(center * center, axis=-1, keepdims=True) + EPS)
    scaled = center * inverse
    return (scaled * gain + shift).astype(BF16), scaled, inverse


def norm_back(up, scaled, inverse, gain):
    w = up * gain
    return inverse * (
        w - jnp.mean(w, axis=-1, keepdims=True) - scaled * jnp.mean(w * scaled, axis=-1, keepdims=True)
    )


def gelu(v):
    c = 0.7978845608028654
    t = jnp.tanh(c * (v + 0.044715 * v * v * v))
    return 0.5 * v * (1.0 + t)


def gelu_back(v):
    c = 0.7978845608028654
    t = jnp.tanh(c * (v + 0.044715 * v * v * v))
    return 0.5 * (1.0 + t) + 0.5 * v * (1.0 - t * t) * c * (1.0 + 3 * 0.044715 * v * v)


def attend(q, k, v, mask):
    outs, lses = [], []
    for h in range(q.shape[1] // HDIM):
        cols = slice(h * HDIM, (h + 1) * HDIM)
        s = jnp.where(mask, dot(q[:, cols], k[:, cols], 1, 1) * SCALE, -1e30)
        m = jnp.max(s, axis=1, keepdims=True)
        e = jnp.exp(s - m)
        total = jnp.sum(e, axis=1, keepdims=True)
        p = (e / total).astype(BF16)
        outs.append(dot(p, v[:, cols]))
        lses.append(m + jnp.log(total))
    return jnp.concatenate(outs, axis=1), jnp.concatenate(lses, axis=1)


def attend_back(q, k, v, mask, lse, ctx, grad):
    dq, dk, dv = [], [], []
    for h in range(q.shape[1] // HDIM):
        cols = slice(h * HDIM, (h + 1) * HDIM)
        s = dot(q[:, cols], k[:, cols], 1, 1) * SCALE
        p = jnp.where(mask, jnp.exp(s - lse[:, h : h + 1]), 0.0)
        dp = dot(grad[:, cols], v[:, cols], 1, 1)
        delta = jnp.sum(grad[:, cols].astype(F32) * ctx[:, cols], axis=1, keepdims=True)
        ds = (p * (dp - delta)).astype(BF16)
        dq.append(dot(ds, k[:, cols]) * SCALE)
        dk.append(dot(ds, q[:, cols], 0, 0) * SCALE)
        dv.append(dot(p.astype(BF16), grad[:, cols], 0, 0))
    cat = lambda parts: jnp.concatenate(parts, axis=1)
    return cat(dq), cat(dk), cat(dv)


def local(
    tokens, slot_pos, lengths, thoughts, ln_gain, ln_shift, w_qkv, qv_bias, w_out, out_bias,
    w_fc, fc_bias, w_proj, proj_bias, cotangent,
):
    n_blk, n_f = lax.axis_size("blk"), lax.axis_size("fsdp")
    H = PARTS
    Q = n_blk // H
    b, f = lax.axis_index("blk"), lax.axis_index("fsdp")
    z, y = b // Q, b % Q
    R, D = tokens.shape[1], tokens.shape[2]
    T = R * n_blk
    W = D // H
    S = D // n_f
    FS = w_proj.shape[0]

    def take(x, i, axis=0):
        return lax.dynamic_index_in_dim(x, i, axis, keepdims=False)

    def shift_h(x, k):
        return lax.ppermute(
            x, "blk", [(((c // Q + k) % H) * Q + c % Q, c) for c in range(n_blk)]
        )

    def shift_q(x, j):
        return lax.ppermute(x, "blk", [((c // Q) * Q + (c % Q + j) % Q, c) for c in range(n_blk)])

    def flip(x, bit):
        return lax.ppermute(x, "fsdp", [(c, c ^ bit) for c in range(n_f)])

    def ag_h(x):
        return jnp.roll(jnp.stack([x] + [shift_h(x, k) for k in range(1, H)]), z, axis=0)

    def ag_q(x):
        return jnp.roll(jnp.stack([x] + [shift_q(x, j) for j in range(1, Q)]), y, axis=0)

    def rs_h(x):
        got = [take(x, z).astype(F32)] + [
            shift_h(take(x, (z - k) % H), k).astype(F32) for k in range(1, H)
        ]
        return (got[0] + got[2]) + (got[1] + got[3])

    def rs_q(x):
        got = [take(x, y).astype(F32)] + [
            shift_q(take(x, (y - j) % Q), j).astype(F32) for j in range(1, Q)
        ]
        return sum(got[1:], got[0])

    def sum_q(x):
        if Q == 2:
            return x + shift_q(x, 1)
        return jnp.sum(ag_q(x), axis=0)

    def sum_h(x):
        return (x + shift_h(x, 2)) + (shift_h(x, 1) + shift_h(x, 3))

    def ag_f(x):
        far = flip(x, 2)
        near = flip(jnp.stack([x, far]), 1)
        return jnp.stack([x, near[0], far, near[1]])

    def rs_f(x):
        near = flip(jnp.stack([x[1], x[3]]).astype(BF16), 1).astype(F32)
        mine = x[0] + near[0]
        far = (x[2] + near[1]).astype(BF16)
        return mine + flip(far, 2).astype(F32)

    def in_order(x):
        near, far = (f % 2) == 1, (f // 2) == 1
        x = [jnp.where(near, x[i ^ 1], x[i]) for i in range(4)]
        return jnp.stack([jnp.where(far, x[i ^ 2], x[i]) for i in range(4)])

    own = tokens[0]
    X = jnp.transpose(ag_q(ag_h(own)), (1, 0, 2, 3))
    small = jnp.concatenate(
        [ln_gain, ln_shift, qv_bias, out_bias[None], proj_bias[None]], axis=0
    )
    part = jnp.concatenate(
        [lax.dynamic_slice_in_dim(w_qkv, i * D + z * W, W, axis=1) for i in range(3)], axis=1
    )
    pad = jnp.concatenate([small, jnp.zeros((8, 3 * W - S), BF16)], axis=1)
    pad = jnp.concatenate([pad, jnp.zeros((8, 3 * W), BF16)], axis=0)
    gathered = in_order(ag_f(jnp.concatenate([part, pad], axis=0)))
    wq = gathered[:, :S].reshape(D, 3 * W)
    small = jnp.transpose(gathered[:, S : S + 8, :S], (1, 0, 2)).reshape(8, D).astype(F32)
    gain1, gain2, shift1, shift2, q_bias, v_bias, o_bias, p_bias = [small[i : i + 1] for i in range(8)]
    qb, vb = (lax.dynamic_slice_in_dim(t, z * W, W, axis=1) for t in (q_bias, v_bias))
    bias3 = jnp.concatenate([qb, jnp.zeros_like(qb), vb], axis=1)
    wo = in_order(ag_f(w_out)).reshape(D, D)
    blocks = [lax.dynamic_slice_in_dim(w_fc, (f ^ i) * FS, FS, axis=1) for i in range(4)]
    wf = in_order([blocks[0]] + [flip(blocks[i], i) for i in range(1, 4)]).reshape(D, FS)
    fb = fc_bias.astype(F32)[None]
    dm_all = ag_f(cotangent[0]).reshape(4 * R, D)

    pos = slot_pos[0]
    ends = jnp.sum(jnp.tril(jnp.ones((lengths.shape[1],) * 2, jnp.int32)) * lengths[0][None], axis=1)

    def start_of(p):
        return jnp.max(jnp.where(ends[None, :] <= p[:, None], ends[None, :], 0), axis=1)

    th = thoughts[0]
    NT = th.shape[0]
    pos_y = take(pos.reshape(H, Q, R), y, 1).reshape(H * R)
    own_pos = take(pos.reshape(n_blk, R), b)

    def mask_of(p):
        return (pos[None, :] <= p[:, None]) & (pos[None, :] >= start_of(p)[:, None])

    mask_lat, mask_y = mask_of(th - 1), mask_of(pos_y)
    src = (pos[None, :] == th[:, None] - 1).astype(BF16)
    tgt = (pos[None, :] == th[:, None]).astype(BF16)
    tgt_y = (pos_y[None, :] == th[:, None]).astype(BF16)
    src_own = (own_pos[None, :] == th[:, None] - 1).astype(F32)
    tgt_own = (own_pos[None, :] == th[:, None]).astype(F32)
    is_th = jnp.sum(tgt, axis=0)[:, None] > 0
    is_th_y = jnp.sum(tgt_y, axis=0)[:, None] > 0
    is_th_own = jnp.sum(tgt_own, axis=0)[:, None] > 0

    X = X.reshape(T, D)
    normed, _, _ = norm(X.astype(F32), gain1, shift1)
    qkv = (dot(normed, wq) + bias3).astype(BF16)
    k0, v0 = qkv[:, W : 2 * W], qkv[:, 2 * W :]

    x_lat = dot(src, X)
    q_lat = dot(src, qkv[:, :W]).astype(BF16)
    ctx_lat, lse_lat = attend(q_lat, k0, v0, mask_lat)
    ctx_lat_all = jnp.transpose(ag_h(ctx_lat.astype(BF16)), (1, 0, 2)).reshape(NT, D)
    mid_lat = x_lat + (dot(ctx_lat_all, wo) + o_bias)
    second_lat, scaled2_lat, inv2_lat = norm(mid_lat, gain2, shift2)
    second_lat_all = ag_f(second_lat).reshape(4 * NT, D)
    hidden_lat = dot(second_lat_all, wf) + fb
    active_lat = gelu(hidden_lat).astype(BF16)
    lat_out = mid_lat + (rs_f(dot(active_lat, w_proj).reshape(4, NT, D)) + p_bias)
    normed_th, scaled_th, inv_th = norm(lat_out, gain1, shift1)
    qkv_th = (dot(normed_th, wq) + bias3).astype(BF16)

    qkv_tok = jnp.where(is_th, dot(tgt, qkv_th, 0, 0).astype(BF16), qkv)
    kt, vt = qkv_tok[:, W : 2 * W], qkv_tok[:, 2 * W :]
    q_y = take(qkv_tok[:, :W].reshape(H, Q, R, W), y, 1).reshape(H * R, W)
    ctx, lse = attend(q_y, kt, vt, mask_y)
    ctx_low = ctx.astype(BF16).reshape(H, R, W)
    got = jnp.stack([take(ctx_low, z)] + [shift_h(take(ctx_low, (z - k) % H), k) for k in range(1, H)])
    ctx_own = jnp.transpose(jnp.roll(got, z, axis=0), (1, 0, 2)).reshape(R, D)
    x_own = jnp.where(is_th_own, exact(tgt_own, lat_out, 0, 0), own.astype(F32))
    mid = x_own + (dot(ctx_own, wo) + o_bias)
    second, scaled2, inv2 = norm(mid, gain2, shift2)
    second_all = ag_f(second).reshape(4 * R, D)
    hidden = dot(second_all, wf) + fb
    active = gelu(hidden).astype(BF16)
    out = mid + (rs_f(dot(active, w_proj).reshape(4, R, D)) + p_bias)

    dh = (dot(dm_all, w_proj, 1, 1) * gelu_back(hidden)).astype(BF16)
    d_second = rs_f(dot(dh, wf, 1, 1).reshape(4, R, D))
    d_mid = cotangent[0].astype(F32) + norm_back(d_second, scaled2, inv2, gain2)
    da = d_mid.astype(BF16)
    d_ctx = dot(da, wo, 1, 1).astype(BF16).reshape(R, H, W)
    got = [take(d_ctx, z, 1)] + [shift_h(take(d_ctx, (z - k) % H, 1), k) for k in range(1, H)]
    grad_y = jnp.roll(jnp.stack(got), z, axis=0).reshape(H * R, W)
    dq, dk, dv = attend_back(q_y, kt, vt, mask_y, lse, ctx, grad_y)
    dq, dk, dv = dq.astype(BF16), dk.astype(BF16), dv.astype(BF16)
    d_th = jnp.concatenate([dot(tgt_y, dq), dot(tgt, dk), dot(tgt, dv)], axis=1).astype(BF16)
    gn_th = dot(d_th, wq, 1, 1)
    up = norm_back(gn_th, scaled_th, inv_th, gain1) + exact(tgt_own, d_mid)
    up = sum_q(up.astype(BF16).astype(F32).astype(BF16).astype(F32)) if Q != 2 else (
        up.astype(BF16).astype(F32) + shift_q(up.astype(BF16), 1).astype(F32)
    )
    up = up.astype(BF16)
    up = (up.astype(F32) + shift_h(up, 2).astype(F32)) + (
        shift_h(up, 1).astype(F32) + shift_h(up, 3).astype(F32)
    )

    dm_lat = up.astype(BF16)
    dm_lat_all = ag_f(dm_lat).reshape(4 * NT, D)
    dh_lat = (dot(dm_lat_all, w_proj, 1, 1) * gelu_back(hidden_lat)).astype(BF16)
    d_second_lat = rs_f(dot(dh_lat, wf, 1, 1).reshape(4, NT, D))
    d_mid_lat = up + norm_back(d_second_lat, scaled2_lat, inv2_lat, gain2)
    da_lat = d_mid_lat.astype(BF16)
    wo_h = take(wo.reshape(H, W, D), z)
    grad_lat = dot(da_lat, wo_h, 1, 1).astype(BF16)
    k_y = take(k0.reshape(H, Q, R, W), y, 1).reshape(H * R, W)
    v_y = take(v0.reshape(H, Q, R, W), y, 1).reshape(H * R, W)
    dq_l, dk_l, dv_l = attend_back(q_lat, k0, v0, mask_lat, lse_lat, ctx_lat, grad_lat)
    dk_l = take(dk_l.reshape(H, Q, R, W), y, 1).reshape(H * R, W)
    dv_l = take(dv_l.reshape(H, Q, R, W), y, 1).reshape(H * R, W)
    src_y = (pos_y[None, :] == th[:, None] - 1).astype(BF16)
    d_lat = jnp.concatenate([dot(src_y, dq_l.astype(BF16), 0, 0), dk_l, dv_l], axis=1)

    kv = jnp.concatenate([dk, dv], axis=1).reshape(H, Q, R, 2 * W)
    d_kv = rs_q(jnp.transpose(kv, (1, 0, 2, 3))).reshape(H * R, 2 * W)
    d_tok = jnp.concatenate([dq.astype(F32), d_kv], axis=1)
    d_all = (jnp.where(is_th_y, 0.0, d_tok) + d_lat).astype(BF16)
    d_tok_th = dot(tgt_y, d_tok.astype(BF16)).astype(BF16)
    normed_y = take(normed.reshape(H, Q, R, D), y, 1).reshape(H * R, D)
    g_q = dot(normed_y, d_all, 0, 0) + dot(normed_th, d_tok_th, 0, 0)
    gn = dot(d_all, wq, 1, 1).astype(BF16).reshape(H, R, D)
    gn_own = rs_h(gn)
    _, scaled1, inv1 = norm(own.astype(F32), gain1, shift1)
    grad_in = jnp.where(is_th_own, 0.0, d_mid) + norm_back(gn_own, scaled1, inv1, gain1)
    grad_in = grad_in + exact(src_own, d_mid_lat, 0, 0)

    da_all = ag_f(da).reshape(4 * R, D)
    ctx_cols = [lax.dynamic_slice_in_dim(ctx_own, (f ^ i) * S, S, axis=1) for i in range(4)]
    ctx_all = jnp.concatenate([ctx_cols[0]] + [flip(ctx_cols[i], i) for i in range(1, 4)], axis=0)
    g_proj = dot(active, dm_all, 0, 0)
    g_fc = dot(second_all, dh, 0, 0)
    g_out = dot(ctx_all, da_all, 0, 0)
    stack = jnp.concatenate(
        [
            g_proj.astype(BF16).reshape(n_blk, FS // n_blk, D),
            jnp.transpose(
                g_fc.astype(BF16).reshape(n_f, n_blk, S // n_blk, FS), (1, 0, 2, 3)
            ).reshape(n_blk, D // n_blk, FS),
            g_out.astype(BF16).reshape(n_blk, S // n_blk, D),
        ],
        axis=1,
    )
    rows = stack.shape[1]
    stack = stack.reshape(H, Q, rows, D)
    mine = rs_h(rs_q(jnp.transpose(stack, (1, 0, 2, 3))).astype(BF16)).astype(BF16)
    c1, c2 = FS // n_blk, FS // n_blk + D // n_blk
    fc_mine = mine[c1:c2].reshape(n_f, S // n_blk, FS)
    fc_cols = in_order(
        [take(fc_mine, f)] + [flip(take(fc_mine, f ^ i), i) for i in range(1, 4)]
    )
    piece = jnp.concatenate([mine[:c1], fc_cols.reshape(D // n_blk, FS), mine[c2:]], axis=0)
    every = jnp.transpose(ag_q(ag_h(piece)), (1, 0, 2, 3)).reshape(n_blk, rows, D)
    w_proj_g = every[:, :c1].reshape(FS, D).astype(F32)
    w_fc_g = jnp.transpose(
        every[:, c1:c2].reshape(n_blk, n_f, S // n_blk, FS), (0, 2, 1, 3)
    ).reshape(S, n_f * FS).astype(F32)
    w_out_g = every[:, c2:].reshape(S, D).astype(F32)
    w_proj_g = w_proj_g + dot(active_lat, dm_lat_all, 0, 0)
    dh_lat_all = in_order(ag_f(dh_lat))
    second_cols = lax.dynamic_slice_in_dim(second_lat_all, f * S, S, axis=1).reshape(4, NT, S)
    parts = []
    for i in range(4):
        order = in_order(second_cols)
        mine_rows = jnp.concatenate([order[i ^ j] for j in range(4)], axis=0)
        parts.append(dot(mine_rows, dh_lat_all[i], 0, 0))
    w_fc_g = w_fc_g + jnp.concatenate(parts, axis=1)
    lat_cols = [lax.dynamic_slice_in_dim(ctx_lat_all, (f ^ i) * S, S, axis=1) for i in range(4)]
    ctx_lat_cols = jnp.concatenate([lat_cols[0]] + [flip(lat_cols[i], i) for i in range(1, 4)], axis=0)
    da_lat_all = ag_f(da_lat).reshape(4 * NT, D)
    w_out_g = w_out_g + dot(ctx_lat_cols, da_lat_all, 0, 0)

    gq = g_q.reshape(4, S, 3 * W)
    gq = rs_f(in_order(gq)).astype(BF16)
    gq = gq.astype(F32) + shift_q(gq, 1).astype(F32) if Q == 2 else sum_q(gq.astype(F32))
    gq = ag_h(gq.astype(BF16))
    w_qkv_g = jnp.transpose(gq.reshape(H, S, 3, W), (1, 2, 0, 3)).reshape(S, 3 * D).astype(F32)

    once = jnp.where(b == 0, 1.0, 0.0)
    col = lambda t: jnp.sum(t.astype(F32), axis=0)
    d_bias = col(d_all) + col(d_tok_th)
    place = lambda v: lax.dynamic_update_slice(jnp.zeros((D,), F32), v, (z * W,))
    gn_f = gn.reshape(H * R, D).astype(F32)
    X_y = take(X.reshape(H, Q, R, D), y, 1).reshape(H * R, D)
    _, scaled_y, _ = norm(X_y.astype(F32), gain1, shift1)
    rows_small = jnp.stack(
        [
            col(gn_f * scaled_y) + col(gn_th * scaled_th),
            col(d_second * scaled2) + once * col(d_second_lat * scaled2_lat),
            col(gn_f) + col(gn_th),
            col(d_second) + once * col(d_second_lat),
            place(d_bias[:W]),
            place(d_bias[2 * W :]),
            col(da) + once * col(da_lat),
            col(cotangent[0]) + once * col(dm_lat),
        ]
    )
    d_fc_bias = lax.dynamic_update_slice(
        jnp.zeros((4, FS), F32), (col(dh) + once * col(dh_lat))[None], (f, 0)
    )
    sums = jnp.concatenate([rows_small, d_fc_bias], axis=0)
    sums = sums + flip(sums, 1)
    sums = sums + flip(sums, 2)
    sums = sum_h(sum_q(sums))
    mine_small = lax.dynamic_slice_in_dim(sums[:8], f * S, S, axis=1)
    return (
        out.astype(BF16)[None],
        grad_in[None],
        mine_small[0:2],
        mine_small[2:4],
        w_qkv_g,
        mine_small[4:6],
        w_out_g,
        mine_small[6],
        w_fc_g,
        take(sums[8:], f),
        w_proj_g,
        mine_small[7],
    )


def solution(mesh):
    a, r, v = P("fsdp", "blk", None), P("fsdp", None), P("fsdp")
    c = P(None, "fsdp")
    return jax.shard_map(
        local,
        mesh=mesh,
        in_specs=(a, r, r, r, c, c, r, c, r, v, r, v, r, v, a),
        out_specs=(a, a, c, c, r, c, r, v, r, v, r, v),
        check_vma=False,
    )
```

time: 1340 us -> 503 us (0.38)
  blocking collectives: 448 us -> 0 us
  waiting for transfers between devices: 581 us -> 160 us
  starting transfers between devices: 1.7 us -> 74.2 us
  matrix products: 156 us -> 88.9 us
  local copies, waits for them, and re-layouts: 70.4 us -> 99 us
  other arithmetic: 44.8 us -> 67.4 us
  between operations: 18.7 us -> 4.18 us
    all_gather x12 -> x0, waiting for transfers between devices: 280 us -> none  [the longest x2 85.9 us: block_forward(): lax.all_gather(value_rows, 'blk', axis=0, tiled=True)]
    psum x1 -> x0, blocking collectives: 279 us -> none  [reduce_once(): return lax.psum(shards, 'blk')]
    ppermute x0 -> x79, waiting for transfers between devices: none -> 160 us  [the longest x30 85.3 us: shift_h(): lax.ppermute(x, 'blk', [((c // Q + k) % H * Q + c % Q, c) for c in range(...]
    all_gather x8 -> x0, blocking collectives: 153 us -> none  [the longest x2 65.3 us: block_backward(): lax.all_gather(logsum, 'blk', axis=1, tiled=True)]
    reduce_scatter x4 -> x0, waiting for transfers between devices: 143 us -> none  [the longest x1 50.3 us: reduce_once(): lax.psum_scatter(gradients[8].astype(jnp.bfloat16), 'fsdp', scatter_dimen...]
    psum x2 -> x0, waiting for transfers between devices: 132 us -> none  [the longest x1 68.6 us: local(): carried = lax.psum(jnp.dot(source, latent_out, precision=highest), 'blk')]
    ppermute x0 -> x79, starting transfers between devices: none -> 74.2 us  [the longest x30 40.6 us: shift_h(): lax.ppermute(x, 'blk', [((c // Q + k) % H * Q + c % Q, c) for c in range(...]
    dot_general x56 -> x73, matrix products: 156 us -> 88.9 us  [the longest x70 85.5 us: dot(): lax.dot_general(a, b, (((ca,), (cb,)), ((), ())), preferred_element_type=...]
  transfers between devices with their start and end apart: 21 -> 79, of which waited for: 15 -> 29; matrix products, arithmetic and copies ran while one was open for 15% -> 47% of each run, Pallas kernels for 0% -> 0%
where the time goes in v1:
time: 503 us; the launch traced here: 494 us
  waiting for transfers between devices  160 us (32%)
  local copies, waits for them, and re-layouts  99 us (20%)
  matrix products  88.9 us (18%)
  starting transfers between devices  74.2 us (15%)
  other arithmetic  67.4 us (13%)
    dot_general x70, matrix products, dot(): lax.dot_general(a, b, (((ca,), (cb,)), ((), ())), preferred_element_type=...  85.5 us
    ppermute x30, waiting for transfers between devices, shift_h(): lax.ppermute(x, 'blk', [((c // Q + k) % H * Q + c % Q, c) for c in range(...  85.3 us
    ppermute x30, starting transfers between devices, shift_h(): lax.ppermute(x, 'blk', [((c // Q + k) % H * Q + c % Q, c) for c in range(...  40.6 us
    ppermute x7, waiting for transfers between devices, shift_q(): lax.ppermute(x, 'blk', [(c // Q * Q + (c % Q + j) % Q, c) for c in range(...  38.2 us
    ppermute x42, waiting for transfers between devices, flip(): return lax.ppermute(x, 'fsdp', [(c, c ^ bit) for c in range(n_f)])  36.6 us
    ppermute x42, starting transfers between devices, flip(): return lax.ppermute(x, 'fsdp', [(c, c ^ bit) for c in range(n_f)])  27.5 us
    concatenate x12, local copies, waits for them, and re-layouts, attend_back(): cat = lambda parts: jnp.concatenate(parts, axis=1)  20.4 us
    unnamed x359, local copies, waits for them, and re-layouts  13.3 us
  transfers between devices with their start and end apart: 79, of which 29 were waited for; matrix products, arithmetic and copies ran while one was open for 47% of the time, Pallas kernels for 0%

profile of v1, /device:TPU:0, one launch (start us, length us, event | category | flops | bytes accessed | tf_op | source)
XLA Modules:
  0.0 493.7 jit_solution(3720876366505126880)
XLA Ops:
  0.7 3.1 collective-permute-start.2
  3.8 2.6 collective-permute-start.1
  48.3 9.8 %collective-permute-done.3 = bf16[4,128,768]{2,1,0:T(8,128)(2,1)} collective-permute-done((bf16[4,128,768]{2,1,0:T(8,128)(2,1)}, bf16[4,128,768]{2,1,0:T(8,128)(2,1)}, u32[]{:S(2)}, u32[]{:S(2)}) %collective-permute-start.3) | collective-permute-done | bytes 786464 | tf_op jit(solution)/shard_map/ppermute | solution.py:104
  69.1 3.0 collective-permute-start.6
  76.8 4.0 collective-permute-done.11
  101.0 3.5 fusion.25
  130.7 4.0 collective-permute-done.21
  149.4 5.6 %collective-permute-done.28 = bf16[128,768]{1,0:T(8,128)(2,1)S(1)} collective-permute-done((bf16[128,768]{1,0:T(8,128)(2,1)S(1)}, bf16[128,768]{1,0:T(8,128)(2,1)S(1)}, u32[]{:S(2)}, u32[]{:S(2)}) %collective-permute-start.28) | collective-permute-done | bytes 196640 | tf_op jit(solution)/shard_map/ppermute | solution.py:107
  155.8 2.5 collective-permute-done.24
  220.1 3.4 concatenate.193
  226.7 2.8 collective-permute-start.35
  234.3 2.5 collective-permute-done.34
  238.6 2.9 collective-permute-done.37
  248.3 2.6 fusion.361
  264.6 5.0 %collective-permute-done.40 = bf16[64,768]{1,0:T(8,128)(2,1)S(1)} collective-permute-done((bf16[64,768]{1,0:T(8,128)(2,1)S(1)}, bf16[64,768]{1,0:T(8,128)(2,1)S(1)}, u32[]{:S(2)}, u32[]{:S(2)}) %collective-permute-start.40) | collective-permute-done | bytes 98336 | tf_op jit(solution)/shard_map/ppermute | solution.py:107
  285.6 2.4 dynamic-slice_reduce_fusion
  289.3 3.0 convert_reduce_fusion.1
  317.7 8.1 %collective-permute-done.47 = f32[12,768]{1,0:T(8,128)S(1)} collective-permute-done((f32[12,768]{1,0:T(8,128)S(1)}, f32[12,768]{1,0:T(8,128)S(1)}, u32[]{:S(2)}, u32[]{:S(2)}) %collective-permute-start.47) | collective-permute-done | bytes 36896 | tf_op jit(solution)/shard_map/ppermute | solution.py:99
  328.0 2.9 collective-permute-done.41
  340.6 7.2 %collective-permute-done.51 = bf16[192,576]{0,1:T(8,128)(2,1)S(1)} collective-permute-done((bf16[192,576]{0,1:T(8,128)(2,1)S(1)}, bf16[192,576]{0,1:T(8,128)(2,1)S(1)}, u32[]{:S(2)}, u32[]{:S(2)}) %collective-permute-start.51) | collective-permute-done | bytes 221216 | tf_op jit(solution)/shard_map/ppermute | solution.py:107
  351.7 5.3 %collective-permute-done.52 = bf16[192,576]{0,1:T(8,128)(2,1)S(1)} collective-permute-done((bf16[192,576]{0,1:T(8,128)(2,1)S(1)}, bf16[192,576]{0,1:T(8,128)(2,1)S(1)}, u32[]{:S(2)}, u32[]{:S(2)}) %collective-permute-start.52) | collective-permute-done | bytes 221216 | tf_op jit(solution)/shard_map/ppermute | solution.py:104
  367.1 3.0 collective-permute-start.62
  370.3 3.6 collective-permute-start.63
  377.2 18.0 %collective-permute-done.62 = bf16[216,768]{1,0:T(8,128)(2,1)S(1)} collective-permute-done((bf16[216,768]{1,0:T(8,128)(2,1)S(1)}, bf16[216,768]{1,0:T(8,128)(2,1)S(1)}, u32[]{:S(2)}, u32[]{:S(2)}) %collective-permute-start.62) | collective-permute-done | bytes 331808 | tf_op jit(solution)/shard_map/ppermute | solution.py:99
  396.5 14.2 %collective-permute-done.54 = bf16[192,576]{0,1:T(8,128)(2,1)S(1)} collective-permute-done((bf16[192,576]{0,1:T(8,128)(2,1)S(1)}, bf16[192,576]{0,1:T(8,128)(2,1)S(1)}, u32[]{:S(2)}, u32[]{:S(2)}) %collective-permute-start.54) | collective-permute-done | bytes 221216 | tf_op jit(solution)/shard_map/ppermute | solution.py:99
  415.9 7.6 %collective-permute-done.55 = bf16[192,576]{0,1:T(8,128)(2,1)S(1)} collective-permute-done((bf16[192,576]{0,1:T(8,128)(2,1)S(1)}, bf16[192,576]{0,1:T(8,128)(2,1)S(1)}, u32[]{:S(2)}, u32[]{:S(2)}) %collective-permute-start.55) | collective-permute-done | bytes 221216 | tf_op jit(solution)/shard_map/ppermute | solution.py:99
  423.7 7.3 %collective-permute-done.68 = bf16[216,768]{1,0:T(8,128)(2,1)S(1)} collective-permute-done((bf16[216,768]{1,0:T(8,128)(2,1)S(1)}, bf16[216,768]{1,0:T(8,128)(2,1)S(1)}, u32[]{:S(2)}, u32[]{:S(2)}) %collective-permute-start.68) | collective-permute-done | bytes 331808 | tf_op jit(solution)/shard_map/ppermute | solution.py:99
  431.0 18.7 %collective-permute-done.69 = bf16[216,768]{1,0:T(8,128)(2,1)S(1)} collective-permute-done((bf16[216,768]{1,0:T(8,128)(2,1)S(1)}, bf16[216,768]{1,0:T(8,128)(2,1)S(1)}, u32[]{:S(2)}, u32[]{:S(2)}) %collective-permute-start.69) | collective-permute-done | bytes 331808 | tf_op jit(solution)/shard_map/ppermute | solution.py:99
  452.4 2.5 copy.121
  454.9 3.7 reshape.737
  460.0 21.5 %collective-permute-done.71 = bf16[4,216,768]{2,1,0:T(8,128)(2,1)} collective-permute-done((bf16[4,216,768]{2,1,0:T(8,128)(2,1)}, bf16[4,216,768]{2,1,0:T(8,128)(2,1)}, u32[]{:S(2)}, u32[]{:S(2)}) %collective-permute-start.71) | collective-permute-done | bytes 1327136 | tf_op jit(solution)/shard_map/ppermute | solution.py:104
  481.5 3.5 fusion.9
  (809 shorter events, 299.7 us)
Async XLA Ops:
  0.7 27.6 %collective-permute-start.2 = (bf16[128,768]{1,0:T(8,128)(2,1)}, bf16[128,768]{1,0:T(8,128)(2,1)}, u32[]{:S(2)}, u32[]{:S(2)}) collective-permute-start(bf16[128,768]{1,0:T(8,128)(2,1)} %bitcast.580), channel_id=1, source_target_pairs={{24,0},{28,4},{0,8},{4,12},{8,16},{12,20},{16,24},{20,28},{25,1},{... | collective-permute-start | bytes 589832 | tf_op jit(solution)/shard_map/ppermute | solution.py:99
  3.8 23.0 %collective-permute-start.1 = (bf16[128,768]{1,0:T(8,128)(2,1)}, bf16[128,768]{1,0:T(8,128)(2,1)}, u32[]{:S(2)}, u32[]{:S(2)}) collective-permute-start(bf16[128,768]{1,0:T(8,128)(2,1)} %bitcast.581), channel_id=1, source_target_pairs={{16,0},{20,4},{24,8},{28,12},{0,16},{4,20},{8,24},{12,28},{17,1},{... | collective-permute-start | bytes 589832 | tf_op jit(solution)/shard_map/ppermute | solution.py:99
  6.4 19.4 %collective-permute-start = (bf16[128,768]{1,0:T(8,128)(2,1)}, bf16[128,768]{1,0:T(8,128)(2,1)}, u32[]{:S(2)}, u32[]{:S(2)}) collective-permute-start(bf16[128,768]{1,0:T(8,128)(2,1)} %bitcast.582), channel_id=1, source_target_pairs={{8,0},{12,4},{16,8},{20,12},{24,16},{28,20},{0,24},{4,28},{9,1},{1... | collective-permute-start | bytes 589832 | tf_op jit(solution)/shard_map/ppermute | solution.py:99
  7.7 15.6 %collective-permute-start.25 = (bf16[128,768]{1,0:T(8,128)(2,1)}, bf16[128,768]{1,0:T(8,128)(2,1)}, u32[]{:S(2)}, u32[]{:S(2)}) collective-permute-start(bf16[128,768]{1,0:T(8,128)(2,1)} %bitcast.601), channel_id=1, source_target_pairs={{0,2},{1,3},{2,0},{3,1},{4,6},{5,7},{6,4},{7,5},{8,10},{9,11},{10,... | collective-permute-start | bytes 589832 | tf_op jit(solution)/shard_map/ppermute | solution.py:107
  13.5 20.9 %collective-permute-start.4 = (bf16[208,576]{1,0:T(8,128)(2,1)}, bf16[208,576]{1,0:T(8,128)(2,1)}, u32[]{:S(2)}, u32[]{:S(2)}) collective-permute-start(bf16[208,576]{1,0:T(8,128)(2,1)} %fusion.134), channel_id=1, source_target_pairs={{0,2},{1,3},{2,0},{3,1},{4,6},{5,7},{6,4},{7,5},{8,10},{9,11},{10,... | collective-permute-start | bytes 718856 | tf_op jit(solution)/shard_map/ppermute | solution.py:107
  25.8 19.8 %collective-permute-start.15 = (bf16[192,768]{1,0:T(8,128)(2,1)}, bf16[192,768]{1,0:T(8,128)(2,1)}, u32[]{:S(2)}, u32[]{:S(2)}) collective-permute-start(bf16[192,768]{1,0:T(8,128)(2,1)} %get-tuple-element.83), channel_id=1, source_target_pairs={{0,1},{1,0},{2,3},{3,2},{4,5},{5,4},{6,7},{7,6},{8,9},{9,8},{10,11... | collective-permute-start | bytes 884744 | tf_op jit(solution)/shard_map/ppermute | solution.py:107
  26.8 18.8 %collective-permute-start.14 = (bf16[192,768]{1,0:T(8,128)(2,1)}, bf16[192,768]{1,0:T(8,128)(2,1)}, u32[]{:S(2)}, u32[]{:S(2)}) collective-permute-start(bf16[192,768]{1,0:T(8,128)(2,1)} %get-tuple-element.84), channel_id=1, source_target_pairs={{0,2},{1,3},{2,0},{3,1},{4,6},{5,7},{6,4},{7,5},{8,10},{9,11},{10,... | collective-permute-start | bytes 884744 | tf_op jit(solution)/shard_map/ppermute | solution.py:107
  38.0 20.1 %collective-permute-start.3 = (bf16[4,128,768]{2,1,0:T(8,128)(2,1)}, bf16[4,128,768]{2,1,0:T(8,128)(2,1)}, u32[]{:S(2)}, u32[]{:S(2)}) collective-permute-start(bf16[4,128,768]{2,1,0:T(8,128)(2,1)} %constant_dynamic-slice_fusion.24), channel_id=1, source_target_pairs={{4,0},{0,4},{12,8},{8,12},{20,16},{16,20},{28,24},{24,28},{5,1},{1... | collective-permute-start | bytes 2359304 | tf_op jit(solution)/shard_map/ppermute | solution.py:104
  91.0 400.3 %collective-permute-start.74 = (bf16[64,192]{1,0:T(8,128)(2,1)}, bf16[64,192]{1,0:T(8,128)(2,1)}, u32[]{:S(2)}, u32[]{:S(2)}) collective-permute-start(bf16[64,192]{1,0:T(8,128)(2,1)} %get-tuple-element.148), channel_id=1, source_target_pairs={{0,3},{1,2},{2,1},{3,0},{4,7},{5,6},{6,5},{7,4},{8,11},{9,10},{10,... | collective-permute-start | bytes 73736 | tf_op jit(solution)/shard_map/ppermute | solution.py:107
  136.7 122.3 %collective-permute-start.58 = (bf16[128,192]{0,1:T(8,128)(2,1)}, bf16[128,192]{0,1:T(8,128)(2,1)}, u32[]{:S(2)}, u32[]{:S(2)}) collective-permute-start(bf16[128,192]{0,1:T(8,128)(2,1)} %get-tuple-element.126), channel_id=1, source_target_pairs={{0,3},{1,2},{2,1},{3,0},{4,7},{5,6},{6,5},{7,4},{8,11},{9,10},{10,... | collective-permute-start | bytes 147464 | tf_op jit(solution)/shard_map/ppermute | solution.py:107
  172.3 57.2 %collective-permute-start.59 = (bf16[128,768]{1,0:T(8,128)(2,1)}, bf16[128,768]{1,0:T(8,128)(2,1)}, u32[]{:S(2)}, u32[]{:S(2)}) collective-permute-start(bf16[128,768]{1,0:T(8,128)(2,1)} %get-tuple-element.61), channel_id=1, source_target_pairs={{0,2},{1,3},{2,0},{3,1},{4,6},{5,7},{6,4},{7,5},{8,10},{9,11},{10,... | collective-permute-start | bytes 589832 | tf_op jit(solution)/shard_map/ppermute | solution.py:107
  207.9 16.7 %collective-permute-start.33 = (bf16[64,768]{1,0:T(8,128)(2,1)}, bf16[64,768]{1,0:T(8,128)(2,1)}, u32[]{:S(2)}, u32[]{:S(2)}) collective-permute-start(bf16[64,768]{1,0:T(8,128)(2,1)} %fusion.44), channel_id=1, source_target_pairs={{4,0},{0,4},{12,8},{8,12},{20,16},{16,20},{28,24},{24,28},{5,1},{1... | collective-permute-start | bytes 294920 | tf_op jit(solution)/shard_map/ppermute | solution.py:104
  232.7 26.6 %collective-permute-start.57 = (bf16[128,192]{0,1:T(8,128)(2,1)}, bf16[128,192]{0,1:T(8,128)(2,1)}, u32[]{:S(2)}, u32[]{:S(2)}) collective-permute-start(bf16[128,192]{0,1:T(8,128)(2,1)} %get-tuple-element.127), channel_id=1, source_target_pairs={{0,2},{1,3},{2,0},{3,1},{4,6},{5,7},{6,4},{7,5},{8,10},{9,11},{10,... | collective-permute-start | bytes 147464 | tf_op jit(solution)/shard_map/ppermute | solution.py:107
  241.5 17.7 %collective-permute-start.56 = (bf16[128,192]{0,1:T(8,128)(2,1)}, bf16[128,192]{0,1:T(8,128)(2,1)}, u32[]{:S(2)}, u32[]{:S(2)}) collective-permute-start(bf16[128,192]{0,1:T(8,128)(2,1)} %get-tuple-element.128), channel_id=1, source_target_pairs={{0,1},{1,0},{2,3},{3,2},{4,5},{5,4},{6,7},{7,6},{8,9},{9,8},{10,11... | collective-permute-start | bytes 147464 | tf_op jit(solution)/shard_map/ppermute | solution.py:107
  255.7 49.9 %collective-permute-start.77 = (bf16[256,768]{1,0:T(8,128)(2,1)}, bf16[256,768]{1,0:T(8,128)(2,1)}, u32[]{:S(2)}, u32[]{:S(2)}) collective-permute-start(bf16[256,768]{1,0:T(8,128)(2,1)} %copy-done.41), channel_id=1, source_target_pairs={{0,2},{1,3},{2,0},{3,1},{4,6},{5,7},{6,4},{7,5},{8,10},{9,11},{10,... | collective-permute-start | bytes 1179656 | tf_op jit(solution)/shard_map/ppermute | solution.py:107
  264.0 101.4 %collective-permute-start.61 = (bf16[4,216,768]{2,1,0:T(8,128)(2,1)}, bf16[4,216,768]{2,1,0:T(8,128)(2,1)}, u32[]{:S(2)}, u32[]{:S(2)}) collective-permute-start(bf16[4,216,768]{2,1,0:T(8,128)(2,1)} %dynamic-slice_bitcast_fusion.1), channel_id=1, source_target_pairs={{4,0},{0,4},{12,8},{8,12},{20,16},{16,20},{28,24},{24,28},{5,1},{1... | collective-permute-start | bytes 3981320 | tf_op jit(solution)/shard_map/ppermute | solution.py:104
  271.8 41.2 %collective-permute-start.75 = (bf16[64,768]{1,0:T(8,128)(2,1)}, bf16[64,768]{1,0:T(8,128)(2,1)}, u32[]{:S(2)}, u32[]{:S(2)}) collective-permute-start(bf16[64,768]{1,0:T(8,128)(2,1)} %get-tuple-element.58), channel_id=1, source_target_pairs={{0,2},{1,3},{2,0},{3,1},{4,6},{5,7},{6,4},{7,5},{8,10},{9,11},{10,... | collective-permute-start | bytes 294920 | tf_op jit(solution)/shard_map/ppermute | solution.py:107
  315.4 15.5 %collective-permute-start.41 = (bf16[128,768]{1,0:T(8,128)(2,1)S(1)}, bf16[128,768]{1,0:T(8,128)(2,1)S(1)}, u32[]{:S(2)}, u32[]{:S(2)}) collective-permute-start(bf16[128,768]{1,0:T(8,128)(2,1)S(1)} %copy-done.89), channel_id=1, source_target_pairs={{16,0},{20,4},{24,8},{28,12},{0,16},{4,20},{8,24},{12,28},{17,1},{... | collective-permute-start | bytes 589832 | tf_op jit(solution)/shard_map/ppermute | solution.py:99
  330.9 18.1 %collective-permute-start.76 = (bf16[2,64,768]{2,1,0:T(8,128)(2,1)}, bf16[2,64,768]{2,1,0:T(8,128)(2,1)}, u32[]{:S(2)}, u32[]{:S(2)}) collective-permute-start(bf16[2,64,768]{2,1,0:T(8,128)(2,1)} %pad_maximum_fusion.31), channel_id=1, source_target_pairs={{0,1},{1,0},{2,3},{3,2},{4,5},{5,4},{6,7},{7,6},{8,9},{9,8},{10,11... | collective-permute-start | bytes 589832 | tf_op jit(solution)/shard_map/ppermute | solution.py:107
  332.4 25.9 %collective-permute-start.78 = (bf16[2,256,768]{2,1,0:T(8,128)(2,1)}, bf16[2,256,768]{2,1,0:T(8,128)(2,1)}, u32[]{:S(2)}, u32[]{:S(2)}) collective-permute-start(bf16[2,256,768]{2,1,0:T(8,128)(2,1)} %pad_maximum_fusion.13), channel_id=1, source_target_pairs={{0,1},{1,0},{2,3},{3,2},{4,5},{5,4},{6,7},{7,6},{8,9},{9,8},{10,11... | collective-permute-start | bytes 2359304 | tf_op jit(solution)/shard_map/ppermute | solution.py:107
  357.0 19.2 %collective-permute-start.53 = (bf16[192,576]{0,1:T(8,128)(2,1)S(1)}, bf16[192,576]{0,1:T(8,128)(2,1)S(1)}, u32[]{:S(2)}, u32[]{:S(2)}) collective-permute-start(bf16[192,576]{0,1:T(8,128)(2,1)S(1)} %get-tuple-element.54), channel_id=1, source_target_pairs={{8,0},{12,4},{16,8},{20,12},{24,16},{28,20},{0,24},{4,28},{9,1},{1... | collective-permute-start | bytes 663560 | tf_op jit(solution)/shard_map/ppermute | solution.py:99
  367.1 28.1 %collective-permute-start.62 = (bf16[216,768]{1,0:T(8,128)(2,1)S(1)}, bf16[216,768]{1,0:T(8,128)(2,1)S(1)}, u32[]{:S(2)}, u32[]{:S(2)}) collective-permute-start(bf16[216,768]{1,0:T(8,128)(2,1)S(1)} %get-tuple-element.80), channel_id=1, source_target_pairs={{16,0},{20,4},{24,8},{28,12},{0,16},{4,20},{8,24},{12,28},{17,1},{... | collective-permute-start | bytes 995336 | tf_op jit(solution)/shard_map/ppermute | solution.py:99
  370.1 25.1 %collective-permute-start.64 = (bf16[216,768]{1,0:T(8,128)(2,1)S(1)}, bf16[216,768]{1,0:T(8,128)(2,1)S(1)}, u32[]{:S(2)}, u32[]{:S(2)}) collective-permute-start(bf16[216,768]{1,0:T(8,128)(2,1)S(1)} %get-tuple-element.81), channel_id=1, source_target_pairs={{24,0},{28,4},{0,8},{4,12},{8,16},{12,20},{16,24},{20,28},{25,1},{... | collective-permute-start | bytes 995336 | tf_op jit(solution)/shard_map/ppermute | solution.py:99
  370.3 24.9 %collective-permute-start.63 = (bf16[216,768]{1,0:T(8,128)(2,1)S(1)}, bf16[216,768]{1,0:T(8,128)(2,1)S(1)}, u32[]{:S(2)}, u32[]{:S(2)}) collective-permute-start(bf16[216,768]{1,0:T(8,128)(2,1)S(1)} %get-tuple-element.82), channel_id=1, source_target_pairs={{8,0},{12,4},{16,8},{20,12},{24,16},{28,20},{0,24},{4,28},{9,1},{1... | collective-permute-start | bytes 995336 | tf_op jit(solution)/shard_map/ppermute | solution.py:99
  376.3 115.1 %collective-permute-start.73 = (bf16[64,192]{1,0:T(8,128)(2,1)}, bf16[64,192]{1,0:T(8,128)(2,1)}, u32[]{:S(2)}, u32[]{:S(2)}) collective-permute-start(bf16[64,192]{1,0:T(8,128)(2,1)} %get-tuple-element.149), channel_id=1, source_target_pairs={{0,2},{1,3},{2,0},{3,1},{4,6},{5,7},{6,4},{7,5},{8,10},{9,11},{10,... | collective-permute-start | bytes 73736 | tf_op jit(solution)/shard_map/ppermute | solution.py:107
  395.2 15.5 %collective-permute-start.54 = (bf16[192,576]{0,1:T(8,128)(2,1)S(1)}, bf16[192,576]{0,1:T(8,128)(2,1)S(1)}, u32[]{:S(2)}, u32[]{:S(2)}) collective-permute-start(bf16[192,576]{0,1:T(8,128)(2,1)S(1)} %get-tuple-element.54), channel_id=1, source_target_pairs={{16,0},{20,4},{24,8},{28,12},{0,16},{4,20},{8,24},{12,28},{17,1},{... | collective-permute-start | bytes 663560 | tf_op jit(solution)/shard_map/ppermute | solution.py:99
  395.5 16.3 %collective-permute-start.66 = (bf16[24,768]{1,0:T(8,128)(2,1)S(1)}, bf16[24,768]{1,0:T(8,128)(2,1)S(1)}, u32[]{:S(2)}, u32[]{:S(2)}) collective-permute-start(bf16[24,768]{1,0:T(8,128)(2,1)S(1)} %get-tuple-element.145), channel_id=1, source_target_pairs={{0,2},{1,3},{2,0},{3,1},{4,6},{5,7},{6,4},{7,5},{8,10},{9,11},{10,... | collective-permute-start | bytes 110600 | tf_op jit(solution)/shard_map/ppermute | solution.py:107
  410.8 80.6 %collective-permute-start.72 = (bf16[64,192]{1,0:T(8,128)(2,1)}, bf16[64,192]{1,0:T(8,128)(2,1)}, u32[]{:S(2)}, u32[]{:S(2)}) collective-permute-start(bf16[64,192]{1,0:T(8,128)(2,1)} %get-tuple-element.150), channel_id=1, source_target_pairs={{0,1},{1,0},{2,3},{3,2},{4,5},{5,4},{6,7},{7,6},{8,9},{9,8},{10,11... | collective-permute-start | bytes 73736 | tf_op jit(solution)/shard_map/ppermute | solution.py:107
  414.2 16.8 %collective-permute-start.68 = (bf16[216,768]{1,0:T(8,128)(2,1)S(1)}, bf16[216,768]{1,0:T(8,128)(2,1)S(1)}, u32[]{:S(2)}, u32[]{:S(2)}) collective-permute-start(bf16[216,768]{1,0:T(8,128)(2,1)S(1)} %pad_maximum_fusion.25), channel_id=1, source_target_pairs={{8,0},{12,4},{16,8},{20,12},{24,16},{28,20},{0,24},{4,28},{9,1},{1... | collective-permute-start | bytes 995336 | tf_op jit(solution)/shard_map/ppermute | solution.py:99
  423.6 26.2 %collective-permute-start.69 = (bf16[216,768]{1,0:T(8,128)(2,1)S(1)}, bf16[216,768]{1,0:T(8,128)(2,1)S(1)}, u32[]{:S(2)}, u32[]{:S(2)}) collective-permute-start(bf16[216,768]{1,0:T(8,128)(2,1)S(1)} %pad_maximum_fusion.25), channel_id=1, source_target_pairs={{16,0},{20,4},{24,8},{28,12},{0,16},{4,20},{8,24},{12,28},{17,1},{... | collective-permute-start | bytes 995336 | tf_op jit(solution)/shard_map/ppermute | solution.py:99
  431.0 18.8 %collective-permute-start.70 = (bf16[216,768]{1,0:T(8,128)(2,1)S(1)}, bf16[216,768]{1,0:T(8,128)(2,1)S(1)}, u32[]{:S(2)}, u32[]{:S(2)}) collective-permute-start(bf16[216,768]{1,0:T(8,128)(2,1)S(1)} %pad_maximum_fusion.25), channel_id=1, source_target_pairs={{24,0},{28,4},{0,8},{4,12},{8,16},{12,20},{16,24},{20,28},{25,1},{... | collective-permute-start | bytes 995336 | tf_op jit(solution)/shard_map/ppermute | solution.py:99
  451.2 30.3 %collective-permute-start.71 = (bf16[4,216,768]{2,1,0:T(8,128)(2,1)}, bf16[4,216,768]{2,1,0:T(8,128)(2,1)}, u32[]{:S(2)}, u32[]{:S(2)}) collective-permute-start(bf16[4,216,768]{2,1,0:T(8,128)(2,1)} %constant_dynamic-slice_fusion.6), channel_id=1, source_target_pairs={{4,0},{0,4},{12,8},{8,12},{20,16},{16,20},{28,24},{24,28},{5,1},{1... | collective-permute-start | bytes 3981320 | tf_op jit(solution)/shard_map/ppermute | solution.py:104
  (213 other events, 1529.3 us)
